TPU v7x, 128 devices: a whole 4x4x4 slice. The times are simulated.
128 devices in a mesh: row: 8 (over x_lo, y), col: 16 (over x_hi, z, core).
Axes of the slice: x: 4 (x_hi: 2, x_lo: 2; x = x_hi * 2 + x_lo), y: 4, z: 4, core: 2. Of those that a mesh axis runs over, the one named last changes fastest.
Arguments:
- inverse: bfloat16 [26624, 26624], P('row', 'col'), may hold values from -6 to 6
- panels: bfloat16 [2, 8192, 512], P(None, 'col'), may hold values from -0.0625 to 0.0625
- block_slot: int32 [208], replicated, may hold values from 0 to 207, as said below
- list_ids: int32 [2, 64], replicated, may hold values from 0 to 207, as said below
Outputs:
- packed_panels: float32 [2, 16384, 512], P(None, ('row', 'col'))
- diag_update: float32 [2, 512, 512], replicated
Inputs may be any that keep to these rules, and one draw needn't show every extreme that they name: block_slot is a permutation of the slots. `list_ids`: each supernode lists distinct blocks; at most 16 of a supernode's listed blocks have slots in one grid row (slot // 26 equal), and in every supernode some grid row holds exactly 16. `list_ids`: in each aligned group of 4 list positions of a supernode, at most 1 listed blocks have slots in one grid column (slot // 13 equal).
All inputs are finite; a program needn't handle non-finite values.
Results may differ from a plain program's by a relative error of at most 0.0003.
Values may be sent and summed in bfloat16 or wider, within the bound.
A program may use at most 128 MiB of HBM per device.

v0:
```python
import jax
import jax.numpy as jnp
from jax import lax
from jax.sharding import PartitionSpec as P

BS = 128


def split_up(array, dim, devices):
    dims = array.shape
    pieces = array.reshape(*dims[:dim], devices, dims[dim] // devices, *dims[dim + 1 :])
    return jnp.moveaxis(pieces, dim, 0)


def sent_and_summed(array, axis, dim):
    pieces = split_up(array, dim, lax.axis_size(axis))
    arrived = lax.all_to_all(pieces, axis, split_axis=0, concat_axis=0, tiled=True)
    return arrived.astype(jnp.float32).sum(axis=0)


def lookup_slots(block_slot, list_ids):
    block_ids = jnp.arange(block_slot.shape[0], dtype=jnp.int32)
    matches = list_ids[..., None] == block_ids
    return jnp.sum(jnp.where(matches, block_slot, 0), axis=-1)


def exact_product(left_rows, right_rows):
    return jnp.dot(left_rows.astype(jnp.float32).T, right_rows, precision=lax.Precision.HIGHEST)


def local(inverse, panels, block_slot, list_ids):
    panel_width = panels.shape[2]
    row_blocks = inverse.shape[0] // BS
    col_blocks = inverse.shape[1] // BS
    listed = list_ids.shape[1]
    grid_rows = lax.axis_size("row")
    grid_cols = lax.axis_size("col")
    max_rows = 2 * listed // grid_rows
    own_rows = max_rows * BS // grid_cols
    shard_len = panels.shape[1] // BS
    slot_cap = (col_blocks + grid_cols - 1) // grid_cols
    my_row = lax.axis_index("row")
    my_col = lax.axis_index("col")
    slots = lookup_slots(block_slot, list_ids)
    grid_row = slots // row_blocks
    local_row = slots % row_blocks
    grid_col = slots // col_blocks
    local_col = slots % col_blocks
    a_blocks = inverse.reshape(row_blocks, BS, col_blocks * BS)
    positions = jnp.arange(listed, dtype=jnp.int32)
    col_ids = jnp.arange(col_blocks, dtype=jnp.int32)
    shard_of = positions // shard_len
    local_pos = my_col * shard_len + jnp.arange(shard_len, dtype=jnp.int32)
    panel_sums = []
    diag_terms = []
    for supernode in range(panels.shape[0]):
        cols_here = grid_col[supernode]
        in_row = grid_row[supernode] == my_row
        chosen_pos = jnp.argsort(jnp.where(in_row, positions, listed + positions), stable=True)[
            :max_rows
        ]
        is_valid = in_row[chosen_pos]
        picked = a_blocks[local_row[supernode][chosen_pos]]
        picked = jnp.where(is_valid[:, None, None], picked, jnp.zeros((), jnp.bfloat16)).reshape(
            max_rows * BS, col_blocks * BS
        )
        local_blocks = panels[supernode].reshape(shard_len, BS, panel_width)
        same_group = (
            (cols_here[:, None] == cols_here[None, :])
            & (shard_of[:, None] == shard_of[None, :])
            & (positions[None, :] < positions[:, None])
        )
        same_rank = jnp.sum(same_group.astype(jnp.int32), axis=1)
        dest_ids = jnp.arange(grid_cols * slot_cap, dtype=jnp.int32)
        send_pick = (
            (cols_here[local_pos] * slot_cap + same_rank[local_pos])[None, :] == dest_ids[:, None]
        ).astype(jnp.bfloat16)
        outgoing = jnp.einsum(
            "mj,jbw->mbw", send_pick, local_blocks, preferred_element_type=jnp.float32
        )
        outgoing = outgoing.astype(jnp.bfloat16).reshape(grid_cols * slot_cap * BS, panel_width)
        incoming = lax.all_to_all(outgoing, "col", split_axis=0, concat_axis=0, tiled=True)
        incoming = incoming.reshape(grid_cols * slot_cap, BS, panel_width)
        mine_here = cols_here == my_col
        to_column = (
            mine_here[:, None] & (local_col[supernode][:, None] == col_ids[None, :])
        ).astype(jnp.float32)
        to_slot = ((shard_of * slot_cap + same_rank)[:, None] == dest_ids[None, :]).astype(
            jnp.float32
        )
        select = jnp.dot(to_column.T, to_slot).astype(jnp.bfloat16)
        chosen = jnp.einsum("kj,jbw->kbw", select, incoming, preferred_element_type=jnp.float32)
        chosen = chosen.astype(jnp.bfloat16).reshape(col_blocks * BS, panel_width)
        place = ((chosen_pos[:, None] == local_pos[None, :]) & is_valid[:, None]).astype(
            jnp.bfloat16
        )
        left_local = jnp.einsum(
            "kj,jbw->kbw", place, local_blocks, preferred_element_type=jnp.float32
        )
        left_local = left_local.reshape(max_rows * BS, panel_width)

        def partial_rows(first_row, row_count, picked=picked, chosen=chosen):
            return jnp.dot(picked, chosen, preferred_element_type=jnp.float32)

        mine_sums = lax.psum_scatter(
            partial_rows(jnp.int32(0), own_rows * lax.axis_size("col")),
            "col",
            scatter_dimension=0,
            tiled=True,
        )
        own_left = sent_and_summed(left_local.astype(jnp.bfloat16), "col", 0).astype(jnp.bfloat16)
        contrib = exact_product(own_left, mine_sums)
        panel_sums.append(mine_sums)
        diag_terms.append(contrib)
    diag_total = lax.psum(jnp.stack(diag_terms), ("row", "col"))
    return (jnp.stack(panel_sums), -diag_total)


def solution(mesh):
    return jax.shard_map(
        local,
        mesh=mesh,
        in_specs=(P("row", "col"), P(None, "col", None), P(), P()),
        out_specs=(P(None, ("row", "col"), None), P()),
        check_vma=False,
    )
```

profile of v0, /device:TPU:1, one launch (start us, length us, event | category | flops | bytes accessed | tf_op | source)
XLA Modules:
  0.0 414.8 jit_solution(4478664436259446148)
XLA Ops:
  11.7 2.5 copy.41
  14.2 9.3 %all-to-all-start.1 = ((bf16[16,128,512]{2,1,0:T(8,128)(2,1)}), bf16[16,128,512]{2,1,0:T(8,128)(2,1)S(1)}, u32[]{:S(2)}, u32[]{:S(2)}) async-start(bf16[16,128,512]{2,1,0:T(8,128)(2,1)} %copy.41), calls=%async_computation.2 | async-start | bytes 4194304 | tf_op jit(solution)/shard_map/all_to_all | solution.py:82
  27.0 8.2 %gather_fusion.7 = bf16[16,128,1664]{2,1,0:T(8,128)(2,1)} fusion(bf16[26,128,1664]{2,1,0:T(8,128)(2,1)} %bitcast.73, s32[1024]{0:T(1024)S(1)} %pad_clamp_fusion), kind=kCustom, calls=%fused_computation.7 | custom fusion | bytes 13631552 | tf_op jit(solution)/shard_map/gather | solution.py:63
  35.2 6.4 %broadcast_select_fusion = bf16[16,128,1664]{2,1,0:T(8,128)(2,1)} fusion(bf16[16,128,1664]{2,1,0:T(8,128)(2,1)} %gather_fusion.7, pred[16]{0:T(512)(128)(4,1)S(1)} %gather_fusion.5), kind=kLoop, calls=%fused_computation.10 | loop fusion | flops 3407872 | bytes 13631504 | tf_op jit(solution)/shard_map/jit(_where)/select_n | solution.py:64
  41.6 10.4 %all-to-all-done.1 = bf16[16,128,512]{2,1,0:T(8,128)(2,1)S(1)} async-done(((bf16[16,128,512]{2,1,0:T(8,128)(2,1)}), bf16[16,128,512]{2,1,0:T(8,128)(2,1)S(1)}, u32[]{:S(2)}, u32[]{:S(2)}) %all-to-all-start.1) | async-done | bytes 2097184 | tf_op jit(solution)/shard_map/all_to_all | solution.py:82
  52.0 2.8 fusion.7
  54.8 2.6 copy.43
  57.4 8.6 %fusion.64 = f32[2048,512]{1,0:T(8,128)} fusion(bf16[2048,1664]{1,0:T(8,128)(2,1)} %bitcast.76, bf16[1664,512]{1,0:T(8,128)(2,1)S(1)} %bitcast.81), kind=kOutput, calls=%fused_computation.117 | convolution fusion | flops 3489660928 | bytes 12713984 | tf_op jit(solution)/shard_map/dot_general | solution.py:103
  68.2 2.5 copy.37
  70.7 7.1 %all-to-all-start = ((bf16[16,128,512]{2,1,0:T(8,128)(2,1)}), bf16[16,128,512]{2,1,0:T(8,128)(2,1)S(1)}, u32[]{:S(2)}, u32[]{:S(2)}) async-start(bf16[16,128,512]{2,1,0:T(8,128)(2,1)} %copy.37), calls=%async_computation | async-start | bytes 4194304 | tf_op jit(solution)/shard_map/all_to_all | solution.py:82
  80.8 8.8 %gather_fusion.2 = bf16[16,128,1664]{2,1,0:T(8,128)(2,1)} fusion(bf16[26,128,1664]{2,1,0:T(8,128)(2,1)} %bitcast.74, s32[1024]{0:T(1024)S(1)} %pad_clamp_fusion.3), kind=kCustom, calls=%fused_computation.2 | custom fusion | bytes 13631552 | tf_op jit(solution)/shard_map/gather | solution.py:63
  90.2 6.4 %broadcast_select_fusion.1 = bf16[16,128,1664]{2,1,0:T(8,128)(2,1)} fusion(bf16[16,128,1664]{2,1,0:T(8,128)(2,1)} %gather_fusion.2, pred[16]{0:T(512)(128)(4,1)S(1)} %gather_fusion), kind=kLoop, calls=%fused_computation.11 | loop fusion | flops 3407872 | bytes 13631504 | tf_op jit(solution)/shard_map/jit(_where)/select_n | solution.py:64
  96.6 9.7 %all-to-all-done = bf16[16,128,512]{2,1,0:T(8,128)(2,1)S(1)} async-done(((bf16[16,128,512]{2,1,0:T(8,128)(2,1)}), bf16[16,128,512]{2,1,0:T(8,128)(2,1)S(1)}, u32[]{:S(2)}, u32[]{:S(2)}) %all-to-all-start) | async-done | bytes 2097184 | tf_op jit(solution)/shard_map/all_to_all | solution.py:82
  106.3 2.8 fusion.4
  109.1 2.6 copy.39
  111.7 8.5 %fusion.63 = f32[2048,512]{1,0:T(8,128)} fusion(bf16[2048,1664]{1,0:T(8,128)(2,1)} %bitcast.75, bf16[1664,512]{1,0:T(8,128)(2,1)S(1)} %bitcast.82), kind=kOutput, calls=%fused_computation.116 | convolution fusion | flops 3489660928 | bytes 12713984 | tf_op jit(solution)/shard_map/dot_general | solution.py:103
  121.2 2.5 copy.47
  123.7 10.4 %all-to-all-start.3 = ((bf16[16,128,512]{2,1,0:T(8,128)(2,1)}), bf16[16,128,512]{2,1,0:T(8,128)(2,1)S(1)}, u32[]{:S(2)}, u32[]{:S(2)}) async-start(bf16[16,128,512]{2,1,0:T(8,128)(2,1)} %copy.47), calls=%async_computation.5 | async-start | bytes 4194304 | tf_op jit(solution)/shard_map/all_to_all | solution.py:17
  137.3 28.3 %all-to-all-done.3 = bf16[16,128,512]{2,1,0:T(8,128)(2,1)S(1)} async-done(((bf16[16,128,512]{2,1,0:T(8,128)(2,1)}), bf16[16,128,512]{2,1,0:T(8,128)(2,1)S(1)}, u32[]{:S(2)}, u32[]{:S(2)}) %all-to-all-start.3) | async-done | bytes 2097184 | tf_op jit(solution)/shard_map/all_to_all | solution.py:17
  165.7 7.6 %all-to-all-start.2 = ((bf16[16,128,512]{2,1,0:T(8,128)(2,1)}), bf16[16,128,512]{2,1,0:T(8,128)(2,1)}, u32[]{:S(2)}, u32[]{:S(2)}) async-start(bf16[16,128,512]{2,1,0:T(8,128)(2,1)} %copy.45), calls=%async_computation.4 | async-start | bytes 4194304 | tf_op jit(solution)/shard_map/all_to_all | solution.py:17
  173.8 28.0 %all-to-all-done.2 = bf16[16,128,512]{2,1,0:T(8,128)(2,1)} async-done(((bf16[16,128,512]{2,1,0:T(8,128)(2,1)}), bf16[16,128,512]{2,1,0:T(8,128)(2,1)}, u32[]{:S(2)}, u32[]{:S(2)}) %all-to-all-start.2) | async-done | bytes 2097184 | tf_op jit(solution)/shard_map/all_to_all | solution.py:17
  205.4 43.9 %reduce-scatter.3.cloned.1.call-done = f32[128,512]{1,0:T(8,128)} async-done(((f32[2048,512]{1,0:T(8,128)}), f32[128,512]{1,0:T(8,128)}) %reduce-scatter.3.cloned.1.call-update) | async-done | bytes 262160 | tf_op jit(solution)/shard_map/reduce_scatter | solution.py:105
  254.2 150.9 %all-reduce.2.cloned.1.call-done = f32[2,512,512]{2,1,0:T(8,128)} async-done(((f32[2,512,512]{2,1,0:T(8,128)}), f32[2,512,512]{2,1,0:T(8,128)}) %all-reduce.2.cloned.1.call-update) | async-done | bytes 2097168 | tf_op jit(solution)/shard_map/psum | solution.py:115
  405.1 3.1 neg.3
  (58 shorter events, 26.9 us)
Async XLA Ops:
  14.2 37.8 %all-to-all-start.1 = ((bf16[16,128,512]{2,1,0:T(8,128)(2,1)}), bf16[16,128,512]{2,1,0:T(8,128)(2,1)S(1)}, u32[]{:S(2)}, u32[]{:S(2)}) async-start(bf16[16,128,512]{2,1,0:T(8,128)(2,1)} %copy.41), calls=%async_computation.2 | async-start | bytes 4194304 | tf_op jit(solution)/shard_map/all_to_all | solution.py:82
  23.5 180.2 %reduce-scatter.5.cloned.1.call-start = ((), (), s32[]{:S(2)}) async-start(), calls=%async_computation.7 | async-start | bytes 4456448 | tf_op jit(solution)/shard_map/reduce_scatter | solution.py:105
  70.7 35.6 %all-to-all-start = ((bf16[16,128,512]{2,1,0:T(8,128)(2,1)}), bf16[16,128,512]{2,1,0:T(8,128)(2,1)S(1)}, u32[]{:S(2)}, u32[]{:S(2)}) async-start(bf16[16,128,512]{2,1,0:T(8,128)(2,1)} %copy.37), calls=%async_computation | async-start | bytes 4194304 | tf_op jit(solution)/shard_map/all_to_all | solution.py:82
  77.8 171.4 %reduce-scatter.3.cloned.1.call-start = ((), (), s32[]{:S(2)}) async-start(), calls=%async_computation.6 | async-start | bytes 4456448 | tf_op jit(solution)/shard_map/reduce_scatter | solution.py:105
  123.7 42.0 %all-to-all-start.3 = ((bf16[16,128,512]{2,1,0:T(8,128)(2,1)}), bf16[16,128,512]{2,1,0:T(8,128)(2,1)S(1)}, u32[]{:S(2)}, u32[]{:S(2)}) async-start(bf16[16,128,512]{2,1,0:T(8,128)(2,1)} %copy.47), calls=%async_computation.5 | async-start | bytes 4194304 | tf_op jit(solution)/shard_map/all_to_all | solution.py:17
  165.7 36.2 %all-to-all-start.2 = ((bf16[16,128,512]{2,1,0:T(8,128)(2,1)}), bf16[16,128,512]{2,1,0:T(8,128)(2,1)}, u32[]{:S(2)}, u32[]{:S(2)}) async-start(bf16[16,128,512]{2,1,0:T(8,128)(2,1)} %copy.45), calls=%async_computation.4 | async-start | bytes 4194304 | tf_op jit(solution)/shard_map/all_to_all | solution.py:17
  173.3 231.9 %all-reduce.2.cloned.1.call-start = ((), (), s32[]{:S(2)}) async-start(), calls=%async_computation.8 | async-start | bytes 4194304 | tf_op jit(solution)/shard_map/psum | solution.py:115
  252.3 0.9 copy-start
  252.3 1.0 copy-start.1
Sparse Core Ops, SparseCore 0:
  66.1 95.6 reduce-scatter.4
  166.4 82.7 reduce-scatter.2
  254.6 150.4 all-reduce.1
where the time goes:
time: 416 us; the launch traced here: 415 us
  waiting for transfers between devices  271 us (65%)
  local copies, waits for them, and re-layouts  39.6 us (10%)
  starting transfers between devices  34.9 us (8%)
  matrix products  29.4 us (7%)
  other arithmetic  25.7 us (6%)
  between operations  13.9 us (3%)
    psum x1, waiting for transfers between devices, local(): diag_total = lax.psum(jnp.stack(diag_terms), ('row', 'col'))  151 us
    all_to_all x2, waiting for transfers between devices, sent_and_summed(): lax.all_to_all(pieces, axis, split_axis=0, concat_axis=0, tiled=True)  56.3 us
    reduce_scatter x2, waiting for transfers between devices, local(): lax.psum_scatter(partial_rows(jnp.int32(0), own_rows * lax.axis_size('col...  43.9 us
    all_to_all x2, waiting for transfers between devices, local(): lax.all_to_all(outgoing, 'col', split_axis=0, concat_axis=0, tiled=True)  20.1 us
    gather x4, local copies, waits for them, and re-layouts, local(): picked = a_blocks[local_row[supernode][chosen_pos]]  18.3 us
    all_to_all x2, starting transfers between devices, sent_and_summed(): lax.all_to_all(pieces, axis, split_axis=0, concat_axis=0, tiled=True)  18 us
    dot_general x2, matrix products, partial_rows(): return jnp.dot(picked, chosen, preferred_element_type=jnp.float32)  17.1 us
    all_to_all x2, starting transfers between devices, local(): lax.all_to_all(outgoing, 'col', split_axis=0, concat_axis=0, tiled=True)  16.4 us
  transfers between devices with their start and end apart: 7, of which 6 were waited for; matrix products, arithmetic and copies ran while one was open for 16% of the time, Pallas kernels for 0%

commit v1 on v0

--- a/solution.py
+++ b/solution.py
@@ -112,7 +112,7 @@
         contrib = exact_product(own_left, mine_sums)
         panel_sums.append(mine_sums)
         diag_terms.append(contrib)
-    diag_total = lax.psum(jnp.stack(diag_terms), ("row", "col"))
+    diag_total = lax.psum(lax.psum(jnp.stack(diag_terms), "col"), "row")
     return (jnp.stack(panel_sums), -diag_total)
 
 

time: 416 us -> 492 us (1.18)
  waiting for transfers between devices: 271 us -> 346 us
    psum x1 -> x2, waiting for transfers between devices: 151 us -> 225 us  [local(): diag_total = lax.psum(lax.psum(jnp.stack(diag_terms), 'col'), 'row')]
  transfers between devices with their start and end apart: 7 -> 8, of which waited for: 6 -> 7; matrix products, arithmetic and copies ran while one was open for 16% -> 14% of each run, Pallas kernels for 0% -> 0%
where the time goes in v1:
time: 492 us; the launch traced here: 488 us
  waiting for transfers between devices  346 us (70%)
  local copies, waits for them, and re-layouts  38.6 us (8%)
  starting transfers between devices  34.9 us (7%)
  matrix products  29.4 us (6%)
  other arithmetic  25.7 us (5%)
  between operations  14 us (3%)
    psum x2, waiting for transfers between devices, local(): diag_total = lax.psum(lax.psum(jnp.stack(diag_terms), 'col'), 'row')  225 us
    all_to_all x2, waiting for transfers between devices, sent_and_summed(): lax.all_to_all(pieces, axis, split_axis=0, concat_axis=0, tiled=True)  56.3 us
    reduce_scatter x2, waiting for transfers between devices, local(): lax.psum_scatter(partial_rows(jnp.int32(0), own_rows * lax.axis_size('col...  43.9 us
    all_to_all x2, waiting for transfers between devices, local(): lax.all_to_all(outgoing, 'col', split_axis=0, concat_axis=0, tiled=True)  20.1 us
    gather x4, local copies, waits for them, and re-layouts, local(): picked = a_blocks[local_row[supernode][chosen_pos]]  18.3 us
    all_to_all x2, starting transfers between devices, sent_and_summed(): lax.all_to_all(pieces, axis, split_axis=0, concat_axis=0, tiled=True)  17.9 us
    dot_general x2, matrix products, partial_rows(): return jnp.dot(picked, chosen, preferred_element_type=jnp.float32)  17.1 us
    all_to_all x2, starting transfers between devices, local(): lax.all_to_all(outgoing, 'col', split_axis=0, concat_axis=0, tiled=True)  16.4 us
  transfers between devices with their start and end apart: 8, of which 7 were waited for; matrix products, arithmetic and copies ran while one was open for 14% of the time, Pallas kernels for 0%

profile of v1, /device:TPU:1, one launch (start us, length us, event | category | flops | bytes accessed | tf_op | source)
XLA Modules:
  0.0 488.2 jit_solution(4170121816032635111)
XLA Ops:
  14.2 9.3 %all-to-all-start.1 = ((bf16[16,128,512]{2,1,0:T(8,128)(2,1)}), bf16[16,128,512]{2,1,0:T(8,128)(2,1)S(1)}, u32[]{:S(2)}, u32[]{:S(2)}) async-start(bf16[16,128,512]{2,1,0:T(8,128)(2,1)} %copy.41), calls=%async_computation.2 | async-start | bytes 4194304 | tf_op jit(solution)/shard_map/all_to_all | solution.py:82
  27.0 8.2 %gather_fusion.7 = bf16[16,128,1664]{2,1,0:T(8,128)(2,1)} fusion(bf16[26,128,1664]{2,1,0:T(8,128)(2,1)} %bitcast.73, s32[1024]{0:T(1024)S(1)} %pad_clamp_fusion), kind=kCustom, calls=%fused_computation.7 | custom fusion | bytes 13631552 | tf_op jit(solution)/shard_map/gather | solution.py:63
  35.2 6.4 %broadcast_select_fusion = bf16[16,128,1664]{2,1,0:T(8,128)(2,1)} fusion(bf16[16,128,1664]{2,1,0:T(8,128)(2,1)} %gather_fusion.7, pred[16]{0:T(512)(128)(4,1)S(1)} %gather_fusion.5), kind=kLoop, calls=%fused_computation.10 | loop fusion | flops 3407872 | bytes 13631504 | tf_op jit(solution)/shard_map/jit(_where)/select_n | solution.py:64
  41.6 10.4 %all-to-all-done.1 = bf16[16,128,512]{2,1,0:T(8,128)(2,1)S(1)} async-done(((bf16[16,128,512]{2,1,0:T(8,128)(2,1)}), bf16[16,128,512]{2,1,0:T(8,128)(2,1)S(1)}, u32[]{:S(2)}, u32[]{:S(2)}) %all-to-all-start.1) | async-done | bytes 2097184 | tf_op jit(solution)/shard_map/all_to_all | solution.py:82
  52.0 2.8 fusion.7
  54.8 2.6 copy.43
  57.4 8.6 %fusion.64 = f32[2048,512]{1,0:T(8,128)} fusion(bf16[2048,1664]{1,0:T(8,128)(2,1)} %bitcast.76, bf16[1664,512]{1,0:T(8,128)(2,1)S(1)} %bitcast.81), kind=kOutput, calls=%fused_computation.117 | convolution fusion | flops 3489660928 | bytes 12713984 | tf_op jit(solution)/shard_map/dot_general | solution.py:103
  68.2 2.5 copy.37
  70.7 7.1 %all-to-all-start = ((bf16[16,128,512]{2,1,0:T(8,128)(2,1)}), bf16[16,128,512]{2,1,0:T(8,128)(2,1)S(1)}, u32[]{:S(2)}, u32[]{:S(2)}) async-start(bf16[16,128,512]{2,1,0:T(8,128)(2,1)} %copy.37), calls=%async_computation | async-start | bytes 4194304 | tf_op jit(solution)/shard_map/all_to_all | solution.py:82
  80.8 8.8 %gather_fusion.2 = bf16[16,128,1664]{2,1,0:T(8,128)(2,1)} fusion(bf16[26,128,1664]{2,1,0:T(8,128)(2,1)} %bitcast.74, s32[1024]{0:T(1024)S(1)} %pad_clamp_fusion.3), kind=kCustom, calls=%fused_computation.2 | custom fusion | bytes 13631552 | tf_op jit(solution)/shard_map/gather | solution.py:63
  90.2 6.4 %broadcast_select_fusion.1 = bf16[16,128,1664]{2,1,0:T(8,128)(2,1)} fusion(bf16[16,128,1664]{2,1,0:T(8,128)(2,1)} %gather_fusion.2, pred[16]{0:T(512)(128)(4,1)S(1)} %gather_fusion), kind=kLoop, calls=%fused_computation.11 | loop fusion | flops 3407872 | bytes 13631504 | tf_op jit(solution)/shard_map/jit(_where)/select_n | solution.py:64
  96.6 9.7 %all-to-all-done = bf16[16,128,512]{2,1,0:T(8,128)(2,1)S(1)} async-done(((bf16[16,128,512]{2,1,0:T(8,128)(2,1)}), bf16[16,128,512]{2,1,0:T(8,128)(2,1)S(1)}, u32[]{:S(2)}, u32[]{:S(2)}) %all-to-all-start) | async-done | bytes 2097184 | tf_op jit(solution)/shard_map/all_to_all | solution.py:82
  106.3 2.8 fusion.4
  109.1 2.6 copy.39
  111.7 8.5 %fusion.63 = f32[2048,512]{1,0:T(8,128)} fusion(bf16[2048,1664]{1,0:T(8,128)(2,1)} %bitcast.75, bf16[1664,512]{1,0:T(8,128)(2,1)S(1)} %bitcast.82), kind=kOutput, calls=%fused_computation.116 | convolution fusion | flops 3489660928 | bytes 12713984 | tf_op jit(solution)/shard_map/dot_general | solution.py:103
  121.2 2.5 copy.47
  123.7 10.4 %all-to-all-start.3 = ((bf16[16,128,512]{2,1,0:T(8,128)(2,1)}), bf16[16,128,512]{2,1,0:T(8,128)(2,1)S(1)}, u32[]{:S(2)}, u32[]{:S(2)}) async-start(bf16[16,128,512]{2,1,0:T(8,128)(2,1)} %copy.47), calls=%async_computation.5 | async-start | bytes 4194304 | tf_op jit(solution)/shard_map/all_to_all | solution.py:17
  137.4 28.3 %all-to-all-done.3 = bf16[16,128,512]{2,1,0:T(8,128)(2,1)S(1)} async-done(((bf16[16,128,512]{2,1,0:T(8,128)(2,1)}), bf16[16,128,512]{2,1,0:T(8,128)(2,1)S(1)}, u32[]{:S(2)}, u32[]{:S(2)}) %all-to-all-start.3) | async-done | bytes 2097184 | tf_op jit(solution)/shard_map/all_to_all | solution.py:17
  165.7 7.5 %all-to-all-start.2 = ((bf16[16,128,512]{2,1,0:T(8,128)(2,1)}), bf16[16,128,512]{2,1,0:T(8,128)(2,1)}, u32[]{:S(2)}, u32[]{:S(2)}) async-start(bf16[16,128,512]{2,1,0:T(8,128)(2,1)} %copy.45), calls=%async_computation.4 | async-start | bytes 4194304 | tf_op jit(solution)/shard_map/all_to_all | solution.py:17
  173.8 28.0 %all-to-all-done.2 = bf16[16,128,512]{2,1,0:T(8,128)(2,1)} async-done(((bf16[16,128,512]{2,1,0:T(8,128)(2,1)}), bf16[16,128,512]{2,1,0:T(8,128)(2,1)}, u32[]{:S(2)}, u32[]{:S(2)}) %all-to-all-start.2) | async-done | bytes 2097184 | tf_op jit(solution)/shard_map/all_to_all | solution.py:17
  205.3 43.8 %reduce-scatter.3.cloned.1.call-done = f32[128,512]{1,0:T(8,128)} async-done(((f32[2048,512]{1,0:T(8,128)}), f32[128,512]{1,0:T(8,128)}) %reduce-scatter.3.cloned.1.call-update) | async-done | bytes 262160 | tf_op jit(solution)/shard_map/reduce_scatter | solution.py:105
  252.4 144.2 %all-reduce.3.cloned.1.call-done = f32[2,512,512]{2,1,0:T(8,128)} async-done(((f32[2,512,512]{2,1,0:T(8,128)}), f32[2,512,512]{2,1,0:T(8,128)}) %all-reduce.3.cloned.1.call-update) | async-done | bytes 2097168 | tf_op jit(solution)/shard_map/psum | solution.py:115
  397.4 81.1 %all-reduce.5.cloned.1.call-done = f32[2,512,512]{2,1,0:T(8,128)} async-done(((f32[2,512,512]{2,1,0:T(8,128)}), f32[2,512,512]{2,1,0:T(8,128)}) %all-reduce.5.cloned.1.call-update) | async-done | bytes 2097168 | tf_op jit(solution)/shard_map/psum | solution.py:115
  478.5 3.1 neg.3
  (61 shorter events, 28.5 us)
Async XLA Ops:
  14.2 37.8 %all-to-all-start.1 = ((bf16[16,128,512]{2,1,0:T(8,128)(2,1)}), bf16[16,128,512]{2,1,0:T(8,128)(2,1)S(1)}, u32[]{:S(2)}, u32[]{:S(2)}) async-start(bf16[16,128,512]{2,1,0:T(8,128)(2,1)} %copy.41), calls=%async_computation.2 | async-start | bytes 4194304 | tf_op jit(solution)/shard_map/all_to_all | solution.py:82
  23.5 180.2 %reduce-scatter.5.cloned.1.call-start = ((), (), s32[]{:S(2)}) async-start(), calls=%async_computation.7 | async-start | bytes 4456448 | tf_op jit(solution)/shard_map/reduce_scatter | solution.py:105
  70.7 35.6 %all-to-all-start = ((bf16[16,128,512]{2,1,0:T(8,128)(2,1)}), bf16[16,128,512]{2,1,0:T(8,128)(2,1)S(1)}, u32[]{:S(2)}, u32[]{:S(2)}) async-start(bf16[16,128,512]{2,1,0:T(8,128)(2,1)} %copy.37), calls=%async_computation | async-start | bytes 4194304 | tf_op jit(solution)/shard_map/all_to_all | solution.py:82
  77.8 171.4 %reduce-scatter.3.cloned.1.call-start = ((), (), s32[]{:S(2)}) async-start(), calls=%async_computation.6 | async-start | bytes 4456448 | tf_op jit(solution)/shard_map/reduce_scatter | solution.py:105
  123.7 42.0 %all-to-all-start.3 = ((bf16[16,128,512]{2,1,0:T(8,128)(2,1)}), bf16[16,128,512]{2,1,0:T(8,128)(2,1)S(1)}, u32[]{:S(2)}, u32[]{:S(2)}) async-start(bf16[16,128,512]{2,1,0:T(8,128)(2,1)} %copy.47), calls=%async_computation.5 | async-start | bytes 4194304 | tf_op jit(solution)/shard_map/all_to_all | solution.py:17
  165.7 36.1 %all-to-all-start.2 = ((bf16[16,128,512]{2,1,0:T(8,128)(2,1)}), bf16[16,128,512]{2,1,0:T(8,128)(2,1)}, u32[]{:S(2)}, u32[]{:S(2)}) async-start(bf16[16,128,512]{2,1,0:T(8,128)(2,1)} %copy.45), calls=%async_computation.4 | async-start | bytes 4194304 | tf_op jit(solution)/shard_map/all_to_all | solution.py:17
  173.2 223.3 %all-reduce.3.cloned.1.call-start = ((), (), s32[]{:S(2)}) async-start(), calls=%async_computation.8 | async-start | bytes 4194304 | tf_op jit(solution)/shard_map/psum | solution.py:115
  252.3 144.3 %copy-start = (f32[128,512]{1,0:T(8,128)S(1)}, f32[128,512]{1,0:T(8,128)}, u32[]{:S(2)}) copy-start(f32[128,512]{1,0:T(8,128)} %reduce-scatter.5.cloned.1.call-done) | copy-start | bytes 786436
  252.3 144.3 %copy-start.1 = (f32[128,512]{1,0:T(8,128)S(1)}, f32[128,512]{1,0:T(8,128)}, u32[]{:S(2)}) copy-start(f32[128,512]{1,0:T(8,128)} %reduce-scatter.3.cloned.1.call-done) | copy-start | bytes 786436
  252.3 226.2 %all-reduce.5.cloned.1.call-start = ((), (), s32[]{:S(2)}) async-start(), calls=%async_computation.9 | async-start | bytes 4194304 | tf_op jit(solution)/shard_map/psum | solution.py:115
Sparse Core Ops, SparseCore 0:
  66.1 95.5 reduce-scatter.4
  166.3 82.8 reduce-scatter.2
  252.4 144.0 all-reduce.2
  398.9 79.5 all-reduce.4
